TPU v7x, 512 devices: a whole 4x8x8 slice. The times are simulated.
512 devices in a mesh: gx: 32 (over z, x), gy: 16 (over y, core).
Axes of the slice: x: 4, y: 8, z: 8, core: 2. Of those that a mesh axis runs over, the one named last changes fastest.
Arguments:
- density: float32 [4, 128, 256, 128], P(None, 'gx', 'gy'), may hold values from 0 to 12, as said below
- rate_table: float32 [4, 9], replicated, may hold values from 0 to 128, as said below
Outputs:
- propagated: float32 [4, 128, 256, 128], P(None, 'gx', 'gy')
- step_entries: float32 [4, 5], replicated
Inputs may be any that keep to these rules, and one draw needn't show every extreme that they name: `density`: every entry is positive. `rate_table`: all entries positive; entry r of a row is the constant cr of the steps.
All inputs are finite; a program needn't handle non-finite values.
Results may differ from a plain program's by a relative error of at most 0.0006.
Values sent between devices are 32-bit elements; how exact they have to be, the bound alone decides.
A program may use at most 64 MiB of HBM per device.

v0:
```python
import jax
import jax.numpy as jnp
from jax import lax
from jax.sharding import PartitionSpec as P

tau_step = 0.01
taylor_terms = 16
squarings = 4


def padded_2(array, sides, width):
    for axis, dim in sides:
        size, length = (lax.axis_size(axis), array.shape[dim])
        up = [(i, (i + 1) % size) for i in range(size - 1)]
        down = [(j, i) for i, j in up]
        last = lax.slice_in_dim(array, length - width, length, axis=dim)
        initial = lax.slice_in_dim(array, 0, width, axis=dim)
        before = lax.ppermute(last, axis, up)
        after = lax.ppermute(initial, axis, down)
        array = jnp.concatenate([before, array, after], axis=dim)
    return array


def shift_down(vector_field):
    return jnp.concatenate([jnp.zeros_like(vector_field[..., :1]), vector_field[..., :-1]], axis=-1)


def shift_up(vector_field):
    return jnp.concatenate([vector_field[..., 1:], jnp.zeros_like(vector_field[..., :1])], axis=-1)


def generator_apply(padded, first_i, first_j, member_rates):
    row_count = padded.shape[0] - 4
    col_count = padded.shape[1] - 2
    lattice_depth = padded.shape[2]
    amount_i = (first_i + jnp.arange(row_count, dtype=jnp.int32)).astype(jnp.float32)[:, None, None]
    amount_j = (first_j + jnp.arange(col_count, dtype=jnp.int32)).astype(jnp.float32)[None, :, None]
    amount_k = jnp.arange(lattice_depth, dtype=jnp.int32).astype(jnp.float32)[None, None, :]
    ratio_j = amount_j / member_rates[7]
    ratio_k = amount_k / member_rates[8]
    make_u = member_rates[0] / (1.0 + ratio_j * ratio_j)
    make_v = member_rates[2] / (1.0 + ratio_k * ratio_k)
    outflow = make_u + member_rates[1] * amount_i + make_v + member_rates[3] * amount_j
    outflow = (
        outflow
        + 0.5 * member_rates[4] * amount_i * (amount_i - 1.0)
        + (member_rates[5] + member_rates[6]) * amount_k
    )
    centre = padded[2:-2, 1:-1]
    inflow = make_u * padded[1:-3, 1:-1]
    inflow = inflow + member_rates[1] * (amount_i + 1.0) * padded[3:-1, 1:-1]
    inflow = inflow + make_v * padded[2:-2, :-2]
    inflow = inflow + member_rates[3] * (amount_j + 1.0) * padded[2:-2, 2:]
    inflow = inflow + 0.5 * member_rates[4] * (amount_i + 2.0) * (amount_i + 1.0) * shift_down(
        padded[4:, 1:-1]
    )
    inflow = inflow + member_rates[5] * (amount_k + 1.0) * shift_up(padded[:-4, 1:-1])
    inflow = inflow + member_rates[6] * (amount_k + 1.0) * shift_up(centre)
    return inflow - outflow * centre


def matrix_exponential(small):
    scaled = small * (tau_step / 2.0**squarings)
    identity = jnp.eye(3, dtype=jnp.float32)
    series = identity + jnp.zeros_like(scaled)
    for term_index in range(taylor_terms, 0, -1):
        series = (
            identity
            + jnp.einsum("...ab,...bc->...ac", scaled, series, precision=lax.Precision.HIGHEST)
            / term_index
        )
    for square_index in range(squarings):
        series = jnp.einsum("...ab,...bc->...ac", series, series, precision=lax.Precision.HIGHEST)
    return series


def expand(values):
    return values[:, None, None, None]


def member_sum(left, right):
    return jnp.sum(left * right, axis=(1, 2, 3))


def shards(density, rate_table):
    row_count = density.shape[1]
    col_count = density.shape[2]
    first_i = lax.axis_index("gx") * row_count
    first_j = lax.axis_index("gy") * col_count
    batched = jax.vmap(generator_apply, in_axes=(0, None, None, 0))

    def shallow_image(vector_field):
        widened = padded_2(vector_field, (("gy", 2),), 1)
        padded = padded_2(widened, (("gx", 1),), 2)
        return batched(padded, first_i, first_j, rate_table)

    image_one = shallow_image(density)

    def inner_sum(left, right):
        return lax.psum(member_sum(left, right), ("gx", "gy"))

    def norm_of(vector_field):
        return jnp.sqrt(lax.psum(member_sum(vector_field, vector_field), ("gx", "gy")))

    basis_scale = jnp.sqrt(lax.psum(member_sum(density, density), ("gx", "gy")))
    basis_zero = density / expand(basis_scale)
    candidate = image_one / expand(basis_scale)
    entry_00 = inner_sum(basis_zero, candidate)
    candidate = candidate - expand(entry_00) * basis_zero
    entry_10 = norm_of(candidate)
    basis_one = candidate / expand(entry_10)
    candidate = shallow_image(basis_one)
    entry_01 = inner_sum(basis_zero, candidate)
    candidate = candidate - expand(entry_01) * basis_zero
    entry_11 = inner_sum(basis_one, candidate)
    candidate = candidate - expand(entry_11) * basis_one
    entry_21 = norm_of(candidate)
    basis_two = candidate / expand(entry_21)
    zeros = jnp.zeros_like(entry_00)
    small = jnp.stack(
        [
            jnp.stack([entry_00, entry_01, zeros], -1),
            jnp.stack([entry_10, entry_11, zeros], -1),
            jnp.stack([zeros, entry_21, zeros], -1),
        ],
        -2,
    )
    propagator = matrix_exponential(small)
    propagated = expand(basis_scale) * (
        expand(propagator[:, 0, 0]) * basis_zero
        + expand(propagator[:, 1, 0]) * basis_one
        + expand(propagator[:, 2, 0]) * basis_two
    )
    step_entries = tau_step * jnp.stack([entry_00, entry_10, entry_01, entry_11, entry_21], -1)
    return (propagated, step_entries)


def solution(mesh):
    in_specs = (P(None, "gx", "gy", None), P())
    out_specs = (P(None, "gx", "gy", None), P())
    return jax.shard_map(shards, mesh=mesh, in_specs=in_specs, out_specs=out_specs, check_vma=False)
```

profile of v0, /device:TPU:1, one launch (start us, length us, event | category | flops | bytes accessed | tf_op | source)
XLA Modules:
  0.0 624.7 jit_solution(18076800326916863573)
XLA Ops:
  0.6 0.9 fusion.70
  1.6 4.6 collective-permute-start
  6.2 5.5 collective-permute-start.1
  11.8 1.0 multiply_reduce_fusion.5
  12.8 0.3 slice_reduce_fusion.7
  13.4 1.3 collective-permute-start.2
  14.7 1.3 collective-permute-start.3
  16.1 106.7 %psum.42 = f32[4]{0:T(128)S(1)} all-reduce(f32[4]{0:T(128)S(1)} %multiply_reduce_fusion.5), channel_id=1, replica_groups=mesh['gx'=32,'gy'=16] {'gx','gy'}, use_global_device_ids=true, to_apply=%region_1.0 | all-reduce | flops 4 | bytes 32 | tf_op jit(solution)/shard_map/psum | solution.py:105
  123.0 0.4 multiply_reduce_fusion.4
  123.4 95.3 %psum.43 = f32[4]{0:T(128)S(1)} all-reduce(f32[4]{0:T(128)S(1)} %get-tuple-element.20), channel_id=1, replica_groups=mesh['gx'=32,'gy'=16] {'gx','gy'}, use_global_device_ids=true, to_apply=%region_3.0 | all-reduce | flops 4 | bytes 32 | tf_op jit(solution)/shard_map/psum | solution.py:100
  218.7 0.2 multiply_reduce_fusion.3
  218.9 93.6 %psum.44 = f32[4]{0:T(128)S(1)} all-reduce(f32[4]{0:T(128)S(1)} %multiply_reduce_fusion.3), channel_id=1, replica_groups=mesh['gx'=32,'gy'=16] {'gx','gy'}, use_global_device_ids=true, to_apply=%region_5.0 | all-reduce | flops 4 | bytes 32 | tf_op jit(solution)/shard_map/psum | solution.py:103
  312.6 3.9 collective-permute-start.4
  316.5 1.9 collective-permute-start.5
  318.4 3.0 collective-permute-done.5
  321.5 3.6 collective-permute-start.6
  325.2 1.3 collective-permute-start.7
  326.6 0.2 collective-permute-done.6
  326.8 3.7 collective-permute-done.7
  330.6 0.4 multiply_reduce_fusion.2
  330.9 98.8 %psum.45 = f32[4]{0:T(128)S(1)} all-reduce(f32[4]{0:T(128)S(1)} %get-tuple-element.18), channel_id=1, replica_groups=mesh['gx'=32,'gy'=16] {'gx','gy'}, use_global_device_ids=true, to_apply=%region_7.0 | all-reduce | flops 4 | bytes 32 | tf_op jit(solution)/shard_map/psum | solution.py:100
  429.7 0.2 multiply_reduce_fusion.1
  429.9 94.7 %psum.46 = f32[4]{0:T(128)S(1)} all-reduce(f32[4]{0:T(128)S(1)} %multiply_reduce_fusion.1), channel_id=1, replica_groups=mesh['gx'=32,'gy'=16] {'gx','gy'}, use_global_device_ids=true, to_apply=%region_9.0 | all-reduce | flops 4 | bytes 32 | tf_op jit(solution)/shard_map/psum | solution.py:100
  524.6 0.2 multiply_reduce_fusion
  524.8 94.7 %psum.47 = f32[4]{0:T(128)S(1)} all-reduce(f32[4]{0:T(128)S(1)} %multiply_reduce_fusion), channel_id=1, replica_groups=mesh['gx'=32,'gy'=16] {'gx','gy'}, use_global_device_ids=true, to_apply=%region_11.0 | all-reduce | flops 4 | bytes 32 | tf_op jit(solution)/shard_map/psum | solution.py:103
  619.5 0.7 copy.11
  620.4 0.2 fusion.14
  620.6 0.2 fusion.13
  620.8 0.2 fusion.12
  620.9 0.2 fusion.11
  621.1 0.2 fusion.10
  621.3 0.2 fusion.9
  621.4 0.2 fusion.8
  621.6 0.2 fusion.7
  621.8 0.2 fusion.6
  622.0 0.2 fusion.5
  622.1 0.2 fusion.4
  622.3 0.2 fusion.3
  622.5 0.2 fusion.2
  622.6 0.2 fusion.1
  622.8 0.2 fusion
  623.0 0.2 convolution_add_fusion
  623.1 0.2 fusion.71
  623.3 0.2 fusion.72
  623.5 0.2 fusion.73
  623.6 0.2 fusion.74
  623.8 0.1 slice_reduce_fusion.2
  623.9 0.8 add_multiply_fusion
  (41 shorter events, 1.1 us)
Async XLA Ops:
  0.6 12.7 %copy-start = (f32[4,4,16,128]{3,2,1,0:T(8,128)S(1)}, f32[4,4,16,128]{3,2,1,0:T(8,128)}, u32[]{:S(2)}) copy-start(f32[4,4,16,128]{3,2,1,0:T(8,128)} %param.2) | copy-start | bytes 393220
  1.6 11.8 %collective-permute-start = (f32[4,4,1,128]{3,2,1,0:T(1,128)S(1)}, f32[4,4,1,128]{3,2,1,0:T(1,128)S(1)}, u32[]{:S(2)}, u32[]{:S(2)}) collective-permute-start(f32[4,4,1,128]{3,2,1,0:T(1,128)S(1)} %get-tuple-element.28), channel_id=1, source_target_pairs={{0,1},{1,2},{2,3},{3,4},{4,5},{5,6},{6,7},{7,8},{8,9},{9,10},{10,1... | collective-permute-start | bytes 24584 | tf_op jit(solution)/shard_map/ppermute | solution.py:18
  6.2 7.2 %collective-permute-start.1 = (f32[4,4,1,128]{3,2,1,0:T(1,128)S(1)}, f32[4,4,1,128]{3,2,1,0:T(1,128)S(1)}, u32[]{:S(2)}, u32[]{:S(2)}) collective-permute-start(f32[4,4,1,128]{3,2,1,0:T(1,128)S(1)} %get-tuple-element.29), channel_id=1, source_target_pairs={{1,0},{2,1},{3,2},{4,3},{5,4},{6,5},{7,6},{8,7},{9,8},{10,9},{11,1... | collective-permute-start | bytes 24584 | tf_op jit(solution)/shard_map/ppermute | solution.py:19
  11.7 1.0 copy-start.1
  13.4 109.5 %collective-permute-start.2 = (f32[4,2,18,128]{3,2,1,0:T(8,128)S(1)}, f32[4,2,18,128]{3,2,1,0:T(8,128)S(1)}, u32[]{:S(2)}, u32[]{:S(2)}) collective-permute-start(f32[4,2,18,128]{3,2,1,0:T(8,128)S(1)} %get-tuple-element.25), channel_id=1, source_target_pairs={{0,16},{16,32},{32,48},{48,64},{64,80},{80,96},{96,112},{112,128},... | collective-permute-start | bytes 221192 | tf_op jit(solution)/shard_map/ppermute | solution.py:18
  14.7 108.2 %collective-permute-start.3 = (f32[4,2,18,128]{3,2,1,0:T(8,128)S(1)}, f32[4,2,18,128]{3,2,1,0:T(8,128)S(1)}, u32[]{:S(2)}, u32[]{:S(2)}) collective-permute-start(f32[4,2,18,128]{3,2,1,0:T(8,128)S(1)} %get-tuple-element.24), channel_id=1, source_target_pairs={{16,0},{32,16},{48,32},{64,48},{80,64},{96,80},{112,96},{128,112},... | collective-permute-start | bytes 221192 | tf_op jit(solution)/shard_map/ppermute | solution.py:19
  312.6 5.9 collective-permute-start.4
  316.5 5.0 collective-permute-start.5
  321.5 5.3 collective-permute-start.6
  325.2 5.4 collective-permute-start.7
where the time goes:
time: 626 us; the launch traced here: 625 us
  blocking collectives  584 us (93%)
  starting transfers between devices  23.5 us (4%)
  waiting for transfers between devices  7.01 us (1%)
    psum x3, blocking collectives, inner_sum(): return lax.psum(member_sum(left, right), ('gx', 'gy'))  289 us
    psum x2, blocking collectives, norm_of(): lax.psum(member_sum(vector_field, vector_field), ('gx', 'gy'))  188 us
    psum x1, blocking collectives, shards(): basis_scale = jnp.sqrt(lax.psum(member_sum(density, density), ('gx', 'gy')))  107 us
    ppermute x4, starting transfers between devices, padded_2(): before = lax.ppermute(last, axis, up)  13.5 us
  transfers between devices with their start and end apart: 8, of which 3 were waited for; matrix products, arithmetic and copies ran while one was open for 0% of the time, Pallas kernels for 0%

commit v1 on v0

v1 whole, which is shorter than its diff:
```python
import functools
import itertools

import jax
import jax.numpy as jnp
from jax import lax
from jax.experimental import pallas as pl
from jax.experimental.pallas import tpu as pltpu
from jax.sharding import PartitionSpec as P

MESH = pl.DeviceIdType.MESH
F32 = jnp.float32
TAU = 0.01
TAYLOR_TERMS = 16
SQUARINGS = 4
M, CI, CJ, NK = 4, 4, 16, 128
NI, NJ = 128, 256
GX, GY = 32, 16
PAIRS = ((0, 0), (0, 1), (0, 2), (1, 1), (1, 2), (2, 2))


def ring(size):
    return sorted(range(1, size), key=lambda a: -min(a, size - a))


def hops_gx(a):
    z, x = a // 4, a % 4
    return min(z, 8 - z) + min(x, 4 - x)


STAGE_GX = sorted(range(1, GX), key=lambda a: -hops_gx(a))
STAGE_GY = ring(GY)


def roll_lanes(value, shift):
    return pltpu.roll(value, shift % NK, value.ndim - 1)


def kernel(
    d_ref, rate_ref, out_ref, entry_ref,
    dpad, upad, from_lo, from_hi, col_out, col_in, cor_out, cor_in, strip,
    rows, total, slots_gx, slots_gy,
    x_send, x_recv, y_send, y_recv, c_send, c_recv, r_send, r_recv,
):
    gx, gy = lax.axis_index("gx"), lax.axis_index("gy")
    first_i, first_j = gx * CI, gy * CJ
    has_x = (gx > 0, gx < GX - 1)
    has_y = (gy > 0, gy < GY - 1)
    step = (-1, 1)

    def at(dx, dy):
        return (gx + dx, gy + dy)

    barrier = pltpu.get_barrier_semaphore()
    for a in STAGE_GX:
        pl.semaphore_signal(barrier, inc=1, device_id=(lax.rem(gx + a, GX), gy), device_id_type=MESH)
    for a in STAGE_GY:
        pl.semaphore_signal(barrier, inc=1, device_id=(gx, lax.rem(gy + a, GY)), device_id_type=MESH)
    for sx, sy in itertools.product((0, 1), (0, 1)):
        @pl.when(has_x[sx] & has_y[sy])
        def _(sx=sx, sy=sy):
            pl.semaphore_signal(barrier, inc=1, device_id=at(step[sx], step[sy]), device_id_type=MESH)

    for sy, (near, far) in enumerate(((0, 1), (CJ - 1, CJ - 2))):
        for m in range(M):
            for r in range(CI):
                col_out[sy, m, r : r + 1] = d_ref[m, r, near : near + 1]
                col_out[sy, m, CI + r : CI + r + 1] = d_ref[m, r, far : far + 1]
            for sx, r0 in enumerate((0, CI - 2)):
                for q in range(2):
                    cor_out[sx, sy, 2 * m + q : 2 * m + q + 1] = d_ref[m, r0 + q, near : near + 1]

    n_x = (gx > 0).astype(jnp.int32) + (gx < GX - 1).astype(jnp.int32)
    n_y = (gy > 0).astype(jnp.int32) + (gy < GY - 1).astype(jnp.int32)
    pl.semaphore_wait(barrier, GX - 1 + GY - 1 + n_x * n_y)

    def x_copy(sx, m):
        dst = (from_hi, from_lo)[sx]
        return pltpu.make_async_remote_copy(
            src_ref=d_ref.at[m], dst_ref=dst.at[m], send_sem=x_send.at[sx, m], recv_sem=x_recv.at[1 - sx, m],
            device_id=at(step[sx], 0), device_id_type=MESH,
        )

    def y_copy(sy):
        return pltpu.make_async_remote_copy(
            src_ref=col_out.at[sy], dst_ref=col_in.at[1 - sy], send_sem=y_send.at[sy], recv_sem=y_recv.at[1 - sy],
            device_id=at(0, step[sy]), device_id_type=MESH,
        )

    def c_copy(sx, sy):
        return pltpu.make_async_remote_copy(
            src_ref=cor_out.at[sx, sy], dst_ref=cor_in.at[1 - sx, 1 - sy],
            send_sem=c_send.at[sx, sy], recv_sem=c_recv.at[1 - sx, 1 - sy],
            device_id=at(step[sx], step[sy]), device_id_type=MESH,
        )

    def incoming_x(sx, m):
        dst = (from_lo, from_hi)[sx]
        return pltpu.make_async_remote_copy(
            src_ref=d_ref.at[m], dst_ref=dst.at[m], send_sem=x_send.at[sx, m], recv_sem=x_recv.at[sx, m],
            device_id=at(step[sx], 0), device_id_type=MESH,
        )

    def incoming_y(sy):
        return pltpu.make_async_remote_copy(
            src_ref=col_out.at[sy], dst_ref=col_in.at[sy], send_sem=y_send.at[sy], recv_sem=y_recv.at[sy],
            device_id=at(0, step[sy]), device_id_type=MESH,
        )

    def incoming_c(sx, sy):
        return pltpu.make_async_remote_copy(
            src_ref=cor_out.at[sx, sy], dst_ref=cor_in.at[sx, sy],
            send_sem=c_send.at[sx, sy], recv_sem=c_recv.at[sx, sy],
            device_id=at(step[sx], step[sy]), device_id_type=MESH,
        )

    for sy in range(2):
        @pl.when(has_y[sy])
        def _(sy=sy):
            y_copy(sy).start()
    for sx, sy in itertools.product((0, 1), (0, 1)):
        @pl.when(has_x[sx] & has_y[sy])
        def _(sx=sx, sy=sy):
            c_copy(sx, sy).start()
    for m in range(M):
        for sx in range(2):
            @pl.when(has_x[sx])
            def _(sx=sx, m=m):
                x_copy(sx, m).start()

    lane = lax.broadcasted_iota(jnp.int32, (1, NK), 1)
    k_row = lane.astype(F32)
    not_first = (lane > 0).astype(F32)
    j_col = (first_j + lax.broadcasted_iota(jnp.int32, (CJ, NK), 0)).astype(F32)
    lam_row = jnp.ones((1, NK), F32)
    rates = []
    for m in range(M):
        c = [rate_ref[m, r] for r in range(9)]
        lam = c[0] + 127.0 * c[1] + c[2] + 255.0 * c[3] + 8001.0 * c[4] + 127.0 * (c[5] + c[6])
        lam_row = jnp.where(lane == m, lam, lam_row)
        rates.append(c)
    inv_row = 1.0 / lam_row

    def coefficients(m):
        inv = inv_row[0, m]
        c = [rates[m][r] * inv for r in range(7)] + rates[m][7:]
        ratio_j = j_col / c[7]
        ratio_k = k_row / c[8]
        make_u = c[0] / (1.0 + ratio_j * ratio_j)
        make_v = c[2] / (1.0 + ratio_k * ratio_k)
        gain_j = c[3] * (j_col + 1.0)
        loss = make_u + make_v + c[3] * j_col + (c[5] + c[6]) * k_row
        return c, make_u, make_v, gain_j, loss

    def row_scalars(c, r):
        i = (first_i + r).astype(F32)
        down = c[1] * (i + 1.0)
        pair = 0.5 * c[4] * (i + 2.0) * (i + 1.0)
        out = c[1] * i + 0.5 * c[4] * i * (i - 1.0)
        return down, pair, out

    def image(c, make_u, make_v, gain_j, loss, scalars, before2, before, here, after, after2, left, right):
        down, pair, out = scalars
        result = make_u * before + down * after + make_v * left + gain_j * right
        result = result + roll_lanes(after2, 1) * (pair * not_first)
        result = result + roll_lanes((c[5] * before2 + c[6] * here) * k_row, -1)
        return result - (loss + out) * here

    for sx in range(2):
        @pl.when(jnp.logical_not(has_x[sx]))
        def _(sx=sx):
            (from_lo, from_hi)[sx][...] = jnp.zeros_like(from_lo)
    for sy in range(2):
        @pl.when(jnp.logical_not(has_y[sy]))
        def _(sy=sy):
            col_in[sy] = jnp.zeros_like(col_in[sy])
    for sx, sy in itertools.product((0, 1), (0, 1)):
        @pl.when(jnp.logical_not(has_x[sx] & has_y[sy]))
        def _(sx=sx, sy=sy):
            cor_in[sx, sy] = jnp.zeros_like(cor_in[sx, sy])

    for m in range(M):
        for r in range(CI):
            dpad[m, r + 2, 8 : 8 + CJ] = d_ref[m, r]

    for sy in range(2):
        @pl.when(has_y[sy])
        def _(sy=sy):
            incoming_y(sy).wait_recv()
    for sx, sy in itertools.product((0, 1), (0, 1)):
        @pl.when(has_x[sx] & has_y[sy])
        def _(sx=sx, sy=sy):
            incoming_c(sx, sy).wait_recv()

    for m in range(M):
        for sy, at_col in enumerate((7, 8 + CJ)):
            for r in range(CI):
                dpad[m, r + 2, at_col : at_col + 1] = col_in[sy, m, r : r + 1]
            strip[m, sy, 2 : 2 + CI] = col_in[sy, m, 0:CI]
            for sx, r0 in enumerate((0, CI + 2)):
                strip[m, sy, r0 : r0 + 2] = cor_in[sx, sy, 2 * m : 2 * m + 2]
                for q in range(2):
                    dpad[m, r0 + q, at_col : at_col + 1] = cor_in[sx, sy, 2 * m + q : 2 * m + q + 1]

    inside_hi = (gx < GX - 1).astype(F32)
    for m in range(M):
        c, make_u, make_v, gain_j, loss = coefficients(m)
        for sx in range(2):
            @pl.when(has_x[sx])
            def _(sx=sx, m=m):
                incoming_x(sx, m).wait_recv()
        for q in range(2):
            dpad[m, q, 8 : 8 + CJ] = from_lo[m, 2 + q]
            dpad[m, CI + 2 + q, 8 : 8 + CJ] = from_hi[m, q]

        def full(r):
            if r < 0:
                return from_lo[m, CI + r]
            if r >= CI:
                return from_hi[m, r - CI]
            return d_ref[m, r]

        for r in range(-2, CI + 2):
            u = image(
                c, make_u, make_v, gain_j, loss, row_scalars(c, r),
                full(r - 2), full(r - 1), full(r), full(r + 1), full(r + 2),
                dpad[m, r + 2, 7 : 7 + CJ], dpad[m, r + 2, 9 : 9 + CJ],
            )
            if r >= CI:
                u = u * inside_hi
            upad[m, r + 2, 8 : 8 + CJ] = u

        i4 = (first_i + lax.broadcasted_iota(jnp.int32, (CI, NK), 0)).astype(F32)
        scalars = (
            c[1] * (i4 + 1.0),
            0.5 * c[4] * (i4 + 2.0) * (i4 + 1.0),
            c[1] * i4 + 0.5 * c[4] * i4 * (i4 - 1.0),
        )
        for sy, (jj, at_col) in enumerate(((-1, 7), (CJ, 8 + CJ))):
            j = jnp.full((1, NK), (first_j + jj).astype(F32))
            ratio = j / c[7]
            mu = c[0] / (1.0 + ratio * ratio)
            lo = mu + make_v + c[3] * j + (c[5] + c[6]) * k_row
            inner, outer = col_out[sy, m, 0:CI], col_in[sy, m, CI : 2 * CI]
            left, right = (outer, inner) if sy == 0 else (inner, outer)
            u = image(
                c, mu, make_v, c[3] * (j + 1.0), lo, scalars,
                strip[m, sy, 0:4], strip[m, sy, 1:5], strip[m, sy, 2:6], strip[m, sy, 3:7], strip[m, sy, 4:8],
                left, right,
            )
            if sy == 1:
                u = u * (gy < GY - 1).astype(F32)
            for r in range(CI):
                upad[m, r + 2, at_col : at_col + 1] = u[r : r + 1]

        sums = [jnp.zeros((8, NK), F32) for _ in PAIRS]
        for r in range(CI):
            mid = lambda q: upad[m, q + 2, 8 : 8 + CJ]
            u2 = image(
                c, make_u, make_v, gain_j, loss, row_scalars(c, r),
                mid(r - 2), mid(r - 1), mid(r), mid(r + 1), mid(r + 2),
                upad[m, r + 2, 7 : 7 + CJ], upad[m, r + 2, 9 : 9 + CJ],
            )
            out_ref[m, r] = u2
            basis = (d_ref[m, r], mid(r), u2)
            for p, (a, b) in enumerate(PAIRS):
                product = basis[a] * basis[b]
                sums[p] = sums[p] + product[0:8] + product[8:16]
        for p in range(len(PAIRS)):
            rows[p * M + m : p * M + m + 1] = jnp.sum(sums[p], axis=0, keepdims=True)

    n_rows = len(PAIRS) * M
    column = jnp.sum(rows[...], axis=1, keepdims=True)
    lanes = lax.broadcasted_iota(jnp.int32, (n_rows, NK), 1)
    places = lax.broadcasted_iota(jnp.int32, (n_rows, NK), 0)
    acc = jnp.sum(jnp.where(lanes == places, column, 0.0), axis=0, keepdims=True)

    for stage, (offsets, slots) in enumerate(((STAGE_GX, slots_gx), (STAGE_GY, slots_gy))):
        total[stage] = acc
        for a in offsets:
            peer = (lax.rem(gx + a, GX), gy) if stage == 0 else (gx, lax.rem(gy + a, GY))
            pltpu.make_async_remote_copy(
                src_ref=total.at[stage], dst_ref=slots.at[a - 1], send_sem=r_send.at[stage], recv_sem=r_recv.at[stage],
                device_id=peer, device_id_type=MESH,
            ).start()
        whole = pltpu.make_async_remote_copy(
            src_ref=slots, dst_ref=slots, send_sem=r_send.at[stage], recv_sem=r_recv.at[stage],
            device_id=(lax.rem(gx + 1, GX), gy), device_id_type=MESH,
        )
        whole.wait_recv()
        acc = acc + jnp.sum(slots[...], axis=0)
        whole.wait_send()

    picked = [acc if p == 0 else roll_lanes(acc, -M * p) for p in range(len(PAIRS))]
    ok = lane < M
    picked = [jnp.where(ok, value, 1.0) for value in picked]
    scale = 1.0 / picked[0]
    a1, a2, b11, b12, b22 = [value * scale for value in picked[1:]]
    h00 = a1
    n1 = b11 - h00 * h00
    h10 = jnp.sqrt(n1)
    e = a2 - h00 * a1
    h01 = e / h10
    h11 = ((b12 - h00 * b11) - h00 * e) / n1
    ss = (b22 - h00 * b12) - h00 * (b12 - h00 * b11)
    h21 = jnp.sqrt(ss / n1 - h01 * h01 - h11 * h11)

    step_scale = lam_row * TAU
    entries = [step_scale * h for h in (h00, h10, h01, h11, h21)]
    small = 1.0 / 2.0**SQUARINGS
    g00, g10, g01, g11, g21 = [entry * small for entry in entries]
    one, zero = jnp.ones_like(h00), jnp.zeros_like(h00)
    p00, p01, p10, p11 = one, zero, zero, one
    w0 = w1 = zero
    for term in range(TAYLOR_TERMS, 0, -1):
        f = 1.0 / term
        w0, w1 = g21 * f * p10, g21 * f * p11
        q00 = 1.0 + (g00 * f * p00 + g01 * f * p10)
        q01 = g00 * f * p01 + g01 * f * p11
        q10 = g10 * f * p00 + g11 * f * p10
        q11 = 1.0 + (g10 * f * p01 + g11 * f * p11)
        p00, p01, p10, p11 = q00, q01, q10, q11
    for _ in range(SQUARINGS):
        w0, w1 = w0 + (w0 * p00 + w1 * p10), w1 + (w0 * p01 + w1 * p11)
        q00 = p00 * p00 + p01 * p10
        q01 = p00 * p01 + p01 * p11
        q10 = p10 * p00 + p11 * p10
        q11 = p10 * p01 + p11 * p11
        p00, p01, p10, p11 = q00, q01, q10, q11
    e0, e1, e2 = p00, p10, w0
    inv10 = 1.0 / h10
    e2 = e2 / h21
    f0 = e0 - e1 * h00 * inv10 + e2 * (h11 * h00 * inv10 - h01)
    f1 = (e1 - e2 * (h00 + h11)) * inv10
    f2 = e2 * inv10

    eye = lax.broadcasted_iota(jnp.int32, (8, NK), 0) == lax.broadcasted_iota(jnp.int32, (8, NK), 1)
    lanes8 = lax.broadcasted_iota(jnp.int32, (8, NK), 1)
    table = jnp.zeros((8, NK), F32)
    for q, entry in enumerate(entries):
        column = jnp.sum(jnp.where(eye, entry, 0.0), axis=1, keepdims=True)
        table = jnp.where(lanes8 == q, column, table)
    entry_ref[...] = table[:M, :5]

    for m in range(M):
        s0, s1, s2 = (jnp.broadcast_to(f[:, m : m + 1], (CJ, NK)) for f in (f0, f1, f2))
        for r in range(CI):
            out_ref[m, r] = s0 * d_ref[m, r] + s1 * upad[m, r + 2, 8 : 8 + CJ] + s2 * out_ref[m, r]

    for sy in range(2):
        @pl.when(has_y[sy])
        def _(sy=sy):
            y_copy(sy).wait_send()
    for sx, sy in itertools.product((0, 1), (0, 1)):
        @pl.when(has_x[sx] & has_y[sy])
        def _(sx=sx, sy=sy):
            c_copy(sx, sy).wait_send()
    for m in range(M):
        for sx in range(2):
            @pl.when(has_x[sx])
            def _(sx=sx, m=m):
                x_copy(sx, m).wait_send()


def shards(density, rate_table):
    vmem = functools.partial(pltpu.VMEM, dtype=F32)
    dma = pltpu.SemaphoreType.DMA
    return pl.pallas_call(
        kernel,
        out_shape=(jax.ShapeDtypeStruct(density.shape, F32), jax.ShapeDtypeStruct((M, 5), F32)),
        in_specs=[pl.BlockSpec(memory_space=pltpu.VMEM), pl.BlockSpec(memory_space=pltpu.SMEM)],
        out_specs=(pl.BlockSpec(memory_space=pltpu.VMEM), pl.BlockSpec(memory_space=pltpu.VMEM)),
        scratch_shapes=[
            vmem((M, CI + 4, 32, NK)),
            vmem((M, CI + 4, 32, NK)),
            vmem((M, CI, CJ, NK)),
            vmem((M, CI, CJ, NK)),
            vmem((2, M, 8, NK)),
            vmem((2, M, 8, NK)),
            vmem((2, 2, 8, NK)),
            vmem((2, 2, 8, NK)),
            vmem((M, 2, 8, NK)),
            vmem((len(PAIRS) * M, NK)),
            vmem((2, 1, NK)),
            vmem((GX - 1, 1, NK)),
            vmem((GY - 1, 1, NK)),
            dma((2, M)),
            dma((2, M)),
            dma((2,)),
            dma((2,)),
            dma((2, 2)),
            dma((2, 2)),
            dma((2,)),
            dma((2,)),
        ],
        compiler_params=pltpu.CompilerParams(collective_id=0, has_side_effects=True),
    )(density, rate_table)


def solution(mesh):
    specs = (P(None, "gx", "gy", None), P())
    return jax.shard_map(shards, mesh=mesh, in_specs=specs, out_specs=specs, check_vma=False)
```

time: 626 us -> 37.3 us (0.06)
  blocking collectives: 584 us -> 0 us
  Pallas kernels: 0 us -> 34.4 us
  starting transfers between devices: 23.5 us -> 0 us
  waiting for transfers between devices: 7.01 us -> 0 us
    psum x6 -> x0, blocking collectives: 584 us -> none  [the longest x3 289 us: inner_sum(): return lax.psum(member_sum(left, right), ('gx', 'gy'))]
    pallas_call x0 -> x1, Pallas kernels: none -> 34.4 us  [shards(): pl.pallas_call(kernel, out_shape=(jax.ShapeDtypeStruct(density.shape, F32...]
    ppermute x8 -> x0, starting transfers between devices: 23.5 us -> none  [the longest x4 13.5 us: padded_2(): before = lax.ppermute(last, axis, up)]
    ppermute x8 -> x0, waiting for transfers between devices: 7.01 us -> none  [the longest x4 6.78 us: padded_2(): after = lax.ppermute(initial, axis, down)]
  transfers between devices with their start and end apart: 8 -> 0, of which waited for: 3 -> 0; matrix products, arithmetic and copies ran while one was open for 0% -> 0% of each run, Pallas kernels for 0% -> 0%
where the time goes in v1:
time: 37.3 us; the launch traced here: 37.2 us
  Pallas kernels  34.4 us (92%)
  local copies, waits for them, and re-layouts  2.15 us (6%)
  between operations  0.65 us (2%)
    pallas_call x1, Pallas kernels, shards(): pl.pallas_call(kernel, out_shape=(jax.ShapeDtypeStruct(density.shape, F32...  34.4 us
    unnamed x4, local copies, waits for them, and re-layouts  2.15 us

profile of v1, /device:TPU:1, one launch (start us, length us, event | category | flops | bytes accessed | tf_op | source)
XLA Modules:
  0.0 37.2 jit_solution(7974757803928711566)
XLA Ops:
  0.6 34.4 %shard_map.41 = (f32[4,4,16,128]{3,2,1,0:T(8,128)}, f32[4,5]{1,0:T(4,128)}) custom-call(f32[4,4,16,128]{3,2,1,0:T(8,128)} %d_ref.1, f32[4,9]{1,0:T(4,128)} %rate_ref.1), custom_call_target="tpu_custom_call" | custom-call | tf_op jit(solution)/shard_map/pallas_call | solution.py:368
  35.0 0.0 copy-start
  35.0 1.6 %copy.6 = f32[4,4,16,128]{3,2,1,0:T(8,128)} copy(f32[4,4,16,128]{3,2,1,0:T(8,128)} %get-tuple-element.4) | data formatting | bytes 262144
  36.6 0.0 copy-done
  36.6 0.6 %copy.7 = f32[4,5]{1,0:T(4,128)} copy(f32[4,5]{1,0:T(4,128)S(1)} %copy-done) | data formatting | bytes 160
Async XLA Ops:
  35.0 1.6 %copy-start = (f32[4,5]{1,0:T(4,128)S(1)}, f32[4,5]{1,0:T(4,128)}, u32[]{:S(2)}) copy-start(f32[4,5]{1,0:T(4,128)} %get-tuple-element.5) | copy-start | bytes 244

commit v2 on v1

--- a/solution.py
+++ b/solution.py
@@ -31,18 +31,30 @@
 STAGE_GX = sorted(range(1, GX), key=lambda a: -hops_gx(a))
 STAGE_GY = ring(GY)
 
+GREETED = (
+    [(0, dx, 0, 0) for dx in (1, 2, 3)]
+    + [(dz, 0, 0, 0) for dz in (1, 2, 6, 7)]
+    + [(0, 0, dy, 0) for dy in (1, 2, 6, 7)]
+    + [(0, 0, 0, 1)]
+)
+TOLD = (
+    [(dz, 0, 0, 0) for dz in (2, 6, 1, 7)] + [(0, 0, dy, 0) for dy in (2, 6, 1, 7)] + [(0, 0, 0, 1)],
+    [(dz, 0, 0, 0) for dz in (4, 3, 5)] + [(0, 0, dy, 0) for dy in (4, 3, 5)],
+)
+
 
 def roll_lanes(value, shift):
     return pltpu.roll(value, shift % NK, value.ndim - 1)
 
 
 def kernel(
-    d_ref, rate_ref, out_ref, entry_ref,
-    dpad, upad, from_lo, from_hi, col_out, col_in, cor_out, cor_in, strip,
+    d_hbm, rate_hbm, out_ref, entry_ref,
+    d_ref, rate_ref, dpad, upad, from_lo, from_hi, col_out, col_in, cor_out, cor_in, strip,
     rows, total, slots_gx, slots_gy,
-    x_send, x_recv, y_send, y_recv, c_send, c_recv, r_send, r_recv,
+    x_send, x_recv, y_send, y_recv, c_send, c_recv, r_send, r_recv, load, known,
 ):
     gx, gy = lax.axis_index("gx"), lax.axis_index("gy")
+    z, x, y, core = lax.div(gx, 4), lax.rem(gx, 4), lax.div(gy, 2), lax.rem(gy, 2)
     first_i, first_j = gx * CI, gy * CJ
     has_x = (gx > 0, gx < GX - 1)
     has_y = (gy > 0, gy < GY - 1)
@@ -51,15 +63,36 @@
     def at(dx, dy):
         return (gx + dx, gy + dy)
 
+    def offset(dz, dx, dy, dc):
+        return (
+            lax.rem(z + dz, GX // 4) * 4 + lax.rem(x + dx, 4),
+            lax.rem(y + dy, GY // 2) * 2 + lax.rem(core + dc, 2),
+        )
+
     barrier = pltpu.get_barrier_semaphore()
-    for a in STAGE_GX:
-        pl.semaphore_signal(barrier, inc=1, device_id=(lax.rem(gx + a, GX), gy), device_id_type=MESH)
-    for a in STAGE_GY:
-        pl.semaphore_signal(barrier, inc=1, device_id=(gx, lax.rem(gy + a, GY)), device_id_type=MESH)
+    for sx in range(2):
+        @pl.when(has_x[sx])
+        def _(sx=sx):
+            pl.semaphore_signal(barrier, inc=1, device_id=at(step[sx], 0), device_id_type=MESH)
+    for sy in range(2):
+        @pl.when(has_y[sy])
+        def _(sy=sy):
+            pl.semaphore_signal(barrier, inc=1, device_id=at(0, step[sy]), device_id_type=MESH)
     for sx, sy in itertools.product((0, 1), (0, 1)):
         @pl.when(has_x[sx] & has_y[sy])
         def _(sx=sx, sy=sy):
             pl.semaphore_signal(barrier, inc=1, device_id=at(step[sx], step[sy]), device_id_type=MESH)
+    for o in GREETED:
+        pl.semaphore_signal(barrier, inc=1, device_id=offset(*o), device_id_type=MESH)
+
+    loads = [
+        pltpu.make_async_copy(d_hbm, d_ref, load.at[0]),
+        pltpu.make_async_copy(rate_hbm, rate_ref, load.at[1]),
+    ]
+    for copy in loads:
+        copy.start()
+    for copy in loads:
+        copy.wait()
 
     for sy, (near, far) in enumerate(((0, 1), (CJ - 1, CJ - 2))):
         for m in range(M):
@@ -72,7 +105,7 @@
 
     n_x = (gx > 0).astype(jnp.int32) + (gx < GX - 1).astype(jnp.int32)
     n_y = (gy > 0).astype(jnp.int32) + (gy < GY - 1).astype(jnp.int32)
-    pl.semaphore_wait(barrier, GX - 1 + GY - 1 + n_x * n_y)
+    pl.semaphore_wait(barrier, len(GREETED) + n_x + n_y + n_x * n_y)
 
     def x_copy(sx, m):
         dst = (from_hi, from_lo)[sx]
@@ -127,6 +160,9 @@
             @pl.when(has_x[sx])
             def _(sx=sx, m=m):
                 x_copy(sx, m).start()
+
+    for o in TOLD[0]:
+        pl.semaphore_signal(known.at[0], inc=1, device_id=offset(*o), device_id_type=MESH)
 
     lane = lax.broadcasted_iota(jnp.int32, (1, NK), 1)
     k_row = lane.astype(F32)
@@ -182,6 +218,10 @@
     for m in range(M):
         for r in range(CI):
             dpad[m, r + 2, 8 : 8 + CJ] = d_ref[m, r]
+
+    pl.semaphore_wait(known.at[0], len(TOLD[0]))
+    for o in TOLD[1]:
+        pl.semaphore_signal(known.at[1], inc=1, device_id=offset(*o), device_id_type=MESH)
 
     for sy in range(2):
         @pl.when(has_y[sy])
@@ -275,6 +315,7 @@
     places = lax.broadcasted_iota(jnp.int32, (n_rows, NK), 0)
     acc = jnp.sum(jnp.where(lanes == places, column, 0.0), axis=0, keepdims=True)
 
+    pl.semaphore_wait(known.at[1], len(TOLD[1]))
     for stage, (offsets, slots) in enumerate(((STAGE_GX, slots_gx), (STAGE_GY, slots_gy))):
         total[stage] = acc
         for a in offsets:
@@ -367,10 +408,12 @@
     dma = pltpu.SemaphoreType.DMA
     return pl.pallas_call(
         kernel,
-        out_shape=(jax.ShapeDtypeStruct(density.shape, F32), jax.ShapeDtypeStruct((M, 5), F32)),
-        in_specs=[pl.BlockSpec(memory_space=pltpu.VMEM), pl.BlockSpec(memory_space=pltpu.SMEM)],
+        out_shape=(pltpu.VMEM(density.shape, F32), pltpu.VMEM((M, 5), F32)),
+        in_specs=[pl.BlockSpec(memory_space=pl.ANY), pl.BlockSpec(memory_space=pl.ANY)],
         out_specs=(pl.BlockSpec(memory_space=pltpu.VMEM), pl.BlockSpec(memory_space=pltpu.VMEM)),
         scratch_shapes=[
+            vmem((M, CI, CJ, NK)),
+            pltpu.SMEM((M, 9), F32),
             vmem((M, CI + 4, 32, NK)),
             vmem((M, CI + 4, 32, NK)),
             vmem((M, CI, CJ, NK)),
@@ -392,6 +435,8 @@
             dma((2, 2)),
             dma((2,)),
             dma((2,)),
+            dma((2,)),
+            pltpu.SemaphoreType.REGULAR((2,)),
         ],
         compiler_params=pltpu.CompilerParams(collective_id=0, has_side_effects=True),
     )(density, rate_table)

time: 37.3 us -> 32.9 us (0.88)
  Pallas kernels: 34.4 us -> 30.9 us
  local copies, waits for them, and re-layouts: 2.15 us -> 1.24 us
    pallas_call x1, Pallas kernels: 34.4 us -> 30.9 us  [shards(): pl.pallas_call(kernel, out_shape=(pltpu.VMEM(density.shape, F32), pltpu.V...]
    unnamed x4 -> x2, local copies, waits for them, and re-layouts: 2.15 us -> 1.24 us
where the time goes in v2:
time: 32.9 us; the launch traced here: 32.8 us
  Pallas kernels  30.9 us (94%)
  local copies, waits for them, and re-layouts  1.24 us (4%)
  between operations  0.64 us (2%)
    pallas_call x1, Pallas kernels, shards(): pl.pallas_call(kernel, out_shape=(pltpu.VMEM(density.shape, F32), pltpu.V...  30.9 us
    unnamed x2, local copies, waits for them, and re-layouts  1.24 us

profile of v2, /device:TPU:1, one launch (start us, length us, event | category | flops | bytes accessed | tf_op | source)
XLA Modules:
  0.0 32.8 jit_solution(4485462815202462689)
XLA Ops:
  0.6 30.9 %shard_map.41 = (f32[4,4,16,128]{3,2,1,0:T(8,128)S(1)}, f32[4,5]{1,0:T(4,128)S(1)}) custom-call(f32[4,4,16,128]{3,2,1,0:T(8,128)} %d_hbm.1, f32[4,9]{1,0:T(4,128)} %rate_hbm.1), custom_call_target="tpu_custom_call" | custom-call | tf_op jit(solution)/shard_map/pallas_call | solution.py:409
  31.6 0.7 %copy.6 = f32[4,4,16,128]{3,2,1,0:T(8,128)} copy(f32[4,4,16,128]{3,2,1,0:T(8,128)S(1)} %get-tuple-element.2) | data formatting | bytes 262144
  32.2 0.6 %copy.7 = f32[4,5]{1,0:T(4,128)} copy(f32[4,5]{1,0:T(4,128)S(1)} %get-tuple-element.3) | data formatting | bytes 160

commit v3 on v2

--- a/solution.py
+++ b/solution.py
@@ -32,14 +32,15 @@
 STAGE_GY = ring(GY)
 
 GREETED = (
-    [(0, dx, 0, 0) for dx in (1, 2, 3)]
-    + [(dz, 0, 0, 0) for dz in (1, 2, 6, 7)]
-    + [(0, 0, dy, 0) for dy in (1, 2, 6, 7)]
+    [(0, dx, 0, 0) for dx in (1, 3)]
+    + [(0, 0, dy, c) for dy in (1, 7) for c in (1, 0)]
+    + [(dz, 0, 0, 0) for dz in (1, 7)]
     + [(0, 0, 0, 1)]
 )
 TOLD = (
-    [(dz, 0, 0, 0) for dz in (2, 6, 1, 7)] + [(0, 0, dy, 0) for dy in (2, 6, 1, 7)] + [(0, 0, 0, 1)],
-    [(dz, 0, 0, 0) for dz in (4, 3, 5)] + [(0, 0, dy, 0) for dy in (4, 3, 5)],
+    GREETED,
+    [(dz, 0, 0, 0) for dz in (2, 6, 1, 7)] + [(0, 0, dy, 0) for dy in (2, 6)],
+    [(dz, 0, 0, 0) for dz in (2, 6)],
 )
 
 
@@ -59,6 +60,7 @@
     has_x = (gx > 0, gx < GX - 1)
     has_y = (gy > 0, gy < GY - 1)
     step = (-1, 1)
+    has_edge = ((x == 0) & has_x[0], (x == 3) & has_x[1])
 
     def at(dx, dy):
         return (gx + dx, gy + dy)
@@ -71,17 +73,9 @@
 
     barrier = pltpu.get_barrier_semaphore()
     for sx in range(2):
-        @pl.when(has_x[sx])
+        @pl.when(has_edge[sx])
         def _(sx=sx):
             pl.semaphore_signal(barrier, inc=1, device_id=at(step[sx], 0), device_id_type=MESH)
-    for sy in range(2):
-        @pl.when(has_y[sy])
-        def _(sy=sy):
-            pl.semaphore_signal(barrier, inc=1, device_id=at(0, step[sy]), device_id_type=MESH)
-    for sx, sy in itertools.product((0, 1), (0, 1)):
-        @pl.when(has_x[sx] & has_y[sy])
-        def _(sx=sx, sy=sy):
-            pl.semaphore_signal(barrier, inc=1, device_id=at(step[sx], step[sy]), device_id_type=MESH)
     for o in GREETED:
         pl.semaphore_signal(barrier, inc=1, device_id=offset(*o), device_id_type=MESH)
 
@@ -103,9 +97,8 @@
                 for q in range(2):
                     cor_out[sx, sy, 2 * m + q : 2 * m + q + 1] = d_ref[m, r0 + q, near : near + 1]
 
-    n_x = (gx > 0).astype(jnp.int32) + (gx < GX - 1).astype(jnp.int32)
-    n_y = (gy > 0).astype(jnp.int32) + (gy < GY - 1).astype(jnp.int32)
-    pl.semaphore_wait(barrier, len(GREETED) + n_x + n_y + n_x * n_y)
+    n_edge = has_edge[0].astype(jnp.int32) + has_edge[1].astype(jnp.int32)
+    pl.semaphore_wait(barrier, len(GREETED) + n_edge)
 
     def x_copy(sx, m):
         dst = (from_hi, from_lo)[sx]
@@ -151,18 +144,17 @@
         @pl.when(has_y[sy])
         def _(sy=sy):
             y_copy(sy).start()
-    for sx, sy in itertools.product((0, 1), (0, 1)):
-        @pl.when(has_x[sx] & has_y[sy])
-        def _(sx=sx, sy=sy):
-            c_copy(sx, sy).start()
     for m in range(M):
         for sx in range(2):
             @pl.when(has_x[sx])
             def _(sx=sx, m=m):
                 x_copy(sx, m).start()
 
-    for o in TOLD[0]:
-        pl.semaphore_signal(known.at[0], inc=1, device_id=offset(*o), device_id_type=MESH)
+    def tell(level):
+        for o in TOLD[level]:
+            pl.semaphore_signal(known.at[level], inc=1, device_id=offset(*o), device_id_type=MESH)
+
+    tell(0)
 
     lane = lax.broadcasted_iota(jnp.int32, (1, NK), 1)
     k_row = lane.astype(F32)
@@ -220,8 +212,13 @@
             dpad[m, r + 2, 8 : 8 + CJ] = d_ref[m, r]
 
     pl.semaphore_wait(known.at[0], len(TOLD[0]))
-    for o in TOLD[1]:
-        pl.semaphore_signal(known.at[1], inc=1, device_id=offset(*o), device_id_type=MESH)
+    for sx, sy in itertools.product((0, 1), (0, 1)):
+        @pl.when(has_x[sx] & has_y[sy])
+        def _(sx=sx, sy=sy):
+            c_copy(sx, sy).start()
+    tell(1)
+    pl.semaphore_wait(known.at[1], len(TOLD[1]))
+    tell(2)
 
     for sy in range(2):
         @pl.when(has_y[sy])
@@ -315,22 +312,24 @@
     places = lax.broadcasted_iota(jnp.int32, (n_rows, NK), 0)
     acc = jnp.sum(jnp.where(lanes == places, column, 0.0), axis=0, keepdims=True)
 
-    pl.semaphore_wait(known.at[1], len(TOLD[1]))
-    for stage, (offsets, slots) in enumerate(((STAGE_GX, slots_gx), (STAGE_GY, slots_gy))):
+    sent = []
+    for stage, (offsets, slots) in enumerate(((STAGE_GY, slots_gy), (STAGE_GX, slots_gx))):
+        if stage == 1:
+            pl.semaphore_wait(known.at[2], len(TOLD[2]))
         total[stage] = acc
         for a in offsets:
-            peer = (lax.rem(gx + a, GX), gy) if stage == 0 else (gx, lax.rem(gy + a, GY))
+            peer = (gx, lax.rem(gy + a, GY)) if stage == 0 else (lax.rem(gx + a, GX), gy)
             pltpu.make_async_remote_copy(
                 src_ref=total.at[stage], dst_ref=slots.at[a - 1], send_sem=r_send.at[stage], recv_sem=r_recv.at[stage],
                 device_id=peer, device_id_type=MESH,
             ).start()
         whole = pltpu.make_async_remote_copy(
             src_ref=slots, dst_ref=slots, send_sem=r_send.at[stage], recv_sem=r_recv.at[stage],
-            device_id=(lax.rem(gx + 1, GX), gy), device_id_type=MESH,
+            device_id=peer, device_id_type=MESH,
         )
         whole.wait_recv()
         acc = acc + jnp.sum(slots[...], axis=0)
-        whole.wait_send()
+        sent.append(whole)
 
     picked = [acc if p == 0 else roll_lanes(acc, -M * p) for p in range(len(PAIRS))]
     ok = lane < M
@@ -388,6 +387,8 @@
         for r in range(CI):
             out_ref[m, r] = s0 * d_ref[m, r] + s1 * upad[m, r + 2, 8 : 8 + CJ] + s2 * out_ref[m, r]
 
+    for whole in sent:
+        whole.wait_send()
     for sy in range(2):
         @pl.when(has_y[sy])
         def _(sy=sy):
@@ -403,10 +404,21 @@
                 x_copy(sx, m).wait_send()
 
 
+def store(field_ref, entry_ref, field_out, entry_out, sems):
+    copies = [
+        pltpu.make_async_copy(field_ref, field_out, sems.at[0]),
+        pltpu.make_async_copy(entry_ref, entry_out, sems.at[1]),
+    ]
+    for copy in copies:
+        copy.start()
+    for copy in copies:
+        copy.wait()
+
+
 def shards(density, rate_table):
     vmem = functools.partial(pltpu.VMEM, dtype=F32)
     dma = pltpu.SemaphoreType.DMA
-    return pl.pallas_call(
+    results = pl.pallas_call(
         kernel,
         out_shape=(pltpu.VMEM(density.shape, F32), pltpu.VMEM((M, 5), F32)),
         in_specs=[pl.BlockSpec(memory_space=pl.ANY), pl.BlockSpec(memory_space=pl.ANY)],
@@ -436,10 +448,18 @@
             dma((2,)),
             dma((2,)),
             dma((2,)),
-            pltpu.SemaphoreType.REGULAR((2,)),
+            pltpu.SemaphoreType.REGULAR((3,)),
         ],
         compiler_params=pltpu.CompilerParams(collective_id=0, has_side_effects=True),
     )(density, rate_table)
+    return pl.pallas_call(
+        store,
+        out_shape=(jax.ShapeDtypeStruct(density.shape, F32), jax.ShapeDtypeStruct((M, 5), F32)),
+        in_specs=[pl.BlockSpec(memory_space=pltpu.VMEM)] * 2,
+        out_specs=(pl.BlockSpec(memory_space=pl.ANY),) * 2,
+        scratch_shapes=[dma((2,))],
+        compiler_params=pltpu.CompilerParams(vmem_limit_bytes=1 << 20),
+    )(*results)
 
 
 def solution(mesh):

time: 32.9 us -> 31.8 us (0.967)
  local copies, waits for them, and re-layouts: 1.24 us -> 0 us
    unnamed x2 -> x0, local copies, waits for them, and re-layouts: 1.24 us -> none
    pallas_call x0 -> x1, Pallas kernels: none -> 0.68 us  [shards(): pl.pallas_call(store, out_shape=(jax.ShapeDtypeStruct(density.shape, F32)...]
    pallas_call x1, Pallas kernels: 30.9 us -> 30.3 us  [shards(): pl.pallas_call(kernel, out_shape=(pltpu.VMEM(density.shape, F32), pltpu.V...]
where the time goes in v3:
time: 31.8 us; the launch traced here: 31.6 us
  Pallas kernels  31 us (97%)
  between operations  0.64 us (2%)
    pallas_call x1, Pallas kernels, shards(): pl.pallas_call(kernel, out_shape=(pltpu.VMEM(density.shape, F32), pltpu.V...  30.3 us
    pallas_call x1, Pallas kernels, shards(): pl.pallas_call(store, out_shape=(jax.ShapeDtypeStruct(density.shape, F32)...  0.68 us

profile of v3, /device:TPU:1, one launch (start us, length us, event | category | flops | bytes accessed | tf_op | source)
XLA Modules:
  0.0 31.6 jit_solution(8512157680485744013)
XLA Ops:
  0.6 30.3 %shard_map.41 = (f32[4,4,16,128]{3,2,1,0:T(8,128)S(1)}, f32[4,5]{1,0:T(4,128)S(1)}) custom-call(f32[4,4,16,128]{3,2,1,0:T(8,128)} %d_hbm.1, f32[4,9]{1,0:T(4,128)} %rate_hbm.1), custom_call_target="tpu_custom_call" | custom-call | tf_op jit(solution)/shard_map/pallas_call | solution.py:421
  31.0 0.7 %shard_map.42 = (f32[4,4,16,128]{3,2,1,0:T(8,128)}, f32[4,5]{1,0:T(4,128)}) custom-call(f32[4,4,16,128]{3,2,1,0:T(8,128)S(1)} %get-tuple-element.4.field_ref, f32[4,5]{1,0:T(4,128)S(1)} %get-tuple-element.5.entry_ref), custom_call_target="tpu_custom_call" | custom-call | tf_op jit(solution)/shard_map/pallas_call | solution.py:455

commit v4 on v3

--- a/solution.py
+++ b/solution.py
@@ -44,6 +44,26 @@
 )
 
 
+FAR_Z = 4
+N_FAR = (GX - 4 * FAR_Z) * GY
+EARLY_REACH = 6
+
+
+def is_early(gx, gy):
+    z, x, y = gx // 4, gx % 4, gy // 2
+    return (5 * y + 2 * x + 4 * z <= EARLY_REACH) & (gx + gy > 0)
+
+
+EARLY = sorted(
+    (p for p in itertools.product(range(GX), range(GY)) if is_early(*p)),
+    key=lambda p: 5 * (p[1] // 2) + 2 * (p[0] % 4) + 4 * (p[0] // 4),
+)
+FAR = sorted(
+    itertools.product(range(4 * FAR_Z, GX), range(GY)),
+    key=lambda p: (abs(p[1] // 2 - 4), abs(p[0] % 4 - 2), p),
+)
+
+
 def roll_lanes(value, shift):
     return pltpu.roll(value, shift % NK, value.ndim - 1)
 
@@ -51,8 +71,8 @@
 def kernel(
     d_hbm, rate_hbm, out_ref, entry_ref,
     d_ref, rate_ref, dpad, upad, from_lo, from_hi, col_out, col_in, cor_out, cor_in, strip,
-    rows, total, slots_gx, slots_gy,
-    x_send, x_recv, y_send, y_recv, c_send, c_recv, r_send, r_recv, load, known,
+    rows, total, slots_gx, slots_gy, direct,
+    x_send, x_recv, y_send, y_recv, c_send, c_recv, r_send, r_recv, e_send, e_recv, load, known,
 ):
     gx, gy = lax.axis_index("gx"), lax.axis_index("gy")
     z, x, y, core = lax.div(gx, 4), lax.rem(gx, 4), lax.div(gy, 2), lax.rem(gy, 2)
@@ -76,8 +96,19 @@
         @pl.when(has_edge[sx])
         def _(sx=sx):
             pl.semaphore_signal(barrier, inc=1, device_id=at(step[sx], 0), device_id_type=MESH)
+    for sx, sy in itertools.product((0, 1), (0, 1)):
+        @pl.when(has_x[sx] & has_y[sy])
+        def _(sx=sx, sy=sy):
+            pl.semaphore_signal(barrier, inc=1, device_id=at(step[sx], step[sy]), device_id_type=MESH)
     for o in GREETED:
         pl.semaphore_signal(barrier, inc=1, device_id=offset(*o), device_id_type=MESH)
+
+    far, early = z >= FAR_Z, is_early(gx, gy)
+
+    @pl.when(early)
+    def _():
+        for p in FAR:
+            pl.semaphore_signal(barrier, inc=1, device_id=p, device_id_type=MESH)
 
     loads = [
         pltpu.make_async_copy(d_hbm, d_ref, load.at[0]),
@@ -88,17 +119,19 @@
     for copy in loads:
         copy.wait()
 
-    for sy, (near, far) in enumerate(((0, 1), (CJ - 1, CJ - 2))):
+    for sy, (near, next_near) in enumerate(((0, 1), (CJ - 1, CJ - 2))):
         for m in range(M):
             for r in range(CI):
                 col_out[sy, m, r : r + 1] = d_ref[m, r, near : near + 1]
-                col_out[sy, m, CI + r : CI + r + 1] = d_ref[m, r, far : far + 1]
+                col_out[sy, m, CI + r : CI + r + 1] = d_ref[m, r, next_near : next_near + 1]
             for sx, r0 in enumerate((0, CI - 2)):
                 for q in range(2):
                     cor_out[sx, sy, 2 * m + q : 2 * m + q + 1] = d_ref[m, r0 + q, near : near + 1]
 
     n_edge = has_edge[0].astype(jnp.int32) + has_edge[1].astype(jnp.int32)
-    pl.semaphore_wait(barrier, len(GREETED) + n_edge)
+    n_x = has_x[0].astype(jnp.int32) + has_x[1].astype(jnp.int32)
+    n_y = has_y[0].astype(jnp.int32) + has_y[1].astype(jnp.int32)
+    pl.semaphore_wait(barrier, len(GREETED) + n_edge + n_x * n_y + far.astype(jnp.int32) * len(EARLY))
 
     def x_copy(sx, m):
         dst = (from_hi, from_lo)[sx]
@@ -144,6 +177,10 @@
         @pl.when(has_y[sy])
         def _(sy=sy):
             y_copy(sy).start()
+    for sx, sy in itertools.product((0, 1), (0, 1)):
+        @pl.when(has_x[sx] & has_y[sy])
+        def _(sx=sx, sy=sy):
+            c_copy(sx, sy).start()
     for m in range(M):
         for sx in range(2):
             @pl.when(has_x[sx])
@@ -212,10 +249,6 @@
             dpad[m, r + 2, 8 : 8 + CJ] = d_ref[m, r]
 
     pl.semaphore_wait(known.at[0], len(TOLD[0]))
-    for sx, sy in itertools.product((0, 1), (0, 1)):
-        @pl.when(has_x[sx] & has_y[sy])
-        def _(sx=sx, sy=sy):
-            c_copy(sx, sy).start()
     tell(1)
     pl.semaphore_wait(known.at[1], len(TOLD[1]))
     tell(2)
@@ -312,24 +345,67 @@
     places = lax.broadcasted_iota(jnp.int32, (n_rows, NK), 0)
     acc = jnp.sum(jnp.where(lanes == places, column, 0.0), axis=0, keepdims=True)
 
-    sent = []
-    for stage, (offsets, slots) in enumerate(((STAGE_GY, slots_gy), (STAGE_GX, slots_gx))):
-        if stage == 1:
-            pl.semaphore_wait(known.at[2], len(TOLD[2]))
-        total[stage] = acc
-        for a in offsets:
-            peer = (gx, lax.rem(gy + a, GY)) if stage == 0 else (lax.rem(gx + a, GX), gy)
-            pltpu.make_async_remote_copy(
-                src_ref=total.at[stage], dst_ref=slots.at[a - 1], send_sem=r_send.at[stage], recv_sem=r_recv.at[stage],
-                device_id=peer, device_id_type=MESH,
-            ).start()
-        whole = pltpu.make_async_remote_copy(
-            src_ref=slots, dst_ref=slots, send_sem=r_send.at[stage], recv_sem=r_recv.at[stage],
-            device_id=peer, device_id_type=MESH,
-        )
-        whole.wait_recv()
-        acc = acc + jnp.sum(slots[...], axis=0)
-        sent.append(whole)
+    total[0] = acc
+
+    def early_copy(p):
+        return pltpu.make_async_remote_copy(
+            src_ref=total.at[0], dst_ref=direct.at[(gx - 4 * FAR_Z) * GY + gy], send_sem=e_send.at[0], recv_sem=e_recv.at[0],
+            device_id=p, device_id_type=MESH,
+        )
+
+    @pl.when(far)
+    def _():
+        for p in EARLY:
+            early_copy(p).start()
+
+    def y_row(a):
+        return pltpu.make_async_remote_copy(
+            src_ref=total.at[0], dst_ref=slots_gy.at[a - 1], send_sem=r_send.at[0], recv_sem=r_recv.at[0],
+            device_id=(gx, lax.rem(gy + a, GY)), device_id_type=MESH,
+        )
+
+    def x_row(a):
+        return pltpu.make_async_remote_copy(
+            src_ref=total.at[1], dst_ref=slots_gx.at[gx], send_sem=r_send.at[1], recv_sem=r_recv.at[1],
+            device_id=(lax.rem(gx + a, GX), gy), device_id_type=MESH,
+        )
+
+    def awaited(rows_ref, send_sem, recv_sem):
+        return pltpu.make_async_remote_copy(
+            src_ref=rows_ref, dst_ref=rows_ref, send_sem=send_sem, recv_sem=recv_sem,
+            device_id=(gx, lax.rem(gy + 1, GY)), device_id_type=MESH,
+        )
+
+    for a in STAGE_GY:
+        y_row(a).start()
+    y_rows = awaited(slots_gy, r_send.at[0], r_recv.at[0])
+    y_rows.wait_recv()
+    acc = acc + jnp.sum(slots_gy[...], axis=0)
+    total[1] = acc
+    slots_gx[gx] = acc
+
+    def wanted(a):
+        return jnp.logical_not(far & is_early(lax.rem(gx + a, GX), gy))
+
+    pl.semaphore_wait(known.at[2], len(TOLD[2]))
+    for a in STAGE_GX:
+        @pl.when(wanted(a))
+        def _(a=a):
+            x_row(a).start()
+
+    @pl.when(early)
+    def _():
+        awaited(slots_gx.at[0 : 4 * FAR_Z - 1], r_send.at[1], r_recv.at[1]).wait_recv()
+        near_sum = jnp.sum(slots_gx[0 : 4 * FAR_Z], axis=0)
+        awaited(direct, e_send.at[0], e_recv.at[0]).wait_recv()
+        total[2] = near_sum + jnp.sum(direct[...], axis=0)
+
+    @pl.when(jnp.logical_not(early))
+    def _():
+        awaited(slots_gx.at[0 : GX - 1], r_send.at[1], r_recv.at[1]).wait_recv()
+        total[2] = jnp.sum(slots_gx[...], axis=0)
+
+    acc = total[2]
 
     picked = [acc if p == 0 else roll_lanes(acc, -M * p) for p in range(len(PAIRS))]
     ok = lane < M
@@ -387,8 +463,21 @@
         for r in range(CI):
             out_ref[m, r] = s0 * d_ref[m, r] + s1 * upad[m, r + 2, 8 : 8 + CJ] + s2 * out_ref[m, r]
 
-    for whole in sent:
-        whole.wait_send()
+    y_rows.wait_send()
+
+    @pl.when(far)
+    def _():
+        for p in EARLY:
+            early_copy(p).wait_send()
+        for a in STAGE_GX:
+            @pl.when(wanted(a))
+            def _(a=a):
+                x_row(a).wait_send()
+
+    @pl.when(jnp.logical_not(far))
+    def _():
+        awaited(slots_gx.at[0 : GX - 1], r_send.at[1], r_recv.at[1]).wait_send()
+
     for sy in range(2):
         @pl.when(has_y[sy])
         def _(sy=sy):
@@ -436,9 +525,10 @@
             vmem((2, 2, 8, NK)),
             vmem((M, 2, 8, NK)),
             vmem((len(PAIRS) * M, NK)),
-            vmem((2, 1, NK)),
-            vmem((GX - 1, 1, NK)),
+            vmem((3, 1, NK)),
+            vmem((GX, 1, NK)),
             vmem((GY - 1, 1, NK)),
+            vmem((N_FAR, 1, NK)),
             dma((2, M)),
             dma((2, M)),
             dma((2,)),
@@ -447,6 +537,8 @@
             dma((2, 2)),
             dma((2,)),
             dma((2,)),
+            dma((1,)),
+            dma((1,)),
             dma((2,)),
             pltpu.SemaphoreType.REGULAR((3,)),
         ],

time: 31.8 us -> 30.6 us (0.962)
  Pallas kernels: 31 us -> 29.8 us
    pallas_call x1, Pallas kernels: 30.3 us -> 29.1 us  [shards(): pl.pallas_call(kernel, out_shape=(pltpu.VMEM(density.shape, F32), pltpu.V...]
where the time goes in v4:
time: 30.6 us; the launch traced here: 30.4 us
  Pallas kernels  29.8 us (97%)
  between operations  0.64 us (2%)
    pallas_call x1, Pallas kernels, shards(): pl.pallas_call(kernel, out_shape=(pltpu.VMEM(density.shape, F32), pltpu.V...  29.1 us
    pallas_call x1, Pallas kernels, shards(): pl.pallas_call(store, out_shape=(jax.ShapeDtypeStruct(density.shape, F32)...  0.68 us

profile of v4, /device:TPU:1, one launch (start us, length us, event | category | flops | bytes accessed | tf_op | source)
XLA Modules:
  0.0 30.4 jit_solution(16566750405169088851)
XLA Ops:
  0.6 29.1 %shard_map.41 = (f32[4,4,16,128]{3,2,1,0:T(8,128)S(1)}, f32[4,5]{1,0:T(4,128)S(1)}) custom-call(f32[4,4,16,128]{3,2,1,0:T(8,128)} %d_hbm.1, f32[4,9]{1,0:T(4,128)} %rate_hbm.1), custom_call_target="tpu_custom_call" | custom-call | tf_op jit(solution)/shard_map/pallas_call | solution.py:510
  29.8 0.7 %shard_map.42 = (f32[4,4,16,128]{3,2,1,0:T(8,128)}, f32[4,5]{1,0:T(4,128)}) custom-call(f32[4,4,16,128]{3,2,1,0:T(8,128)S(1)} %get-tuple-element.4.field_ref, f32[4,5]{1,0:T(4,128)S(1)} %get-tuple-element.5.entry_ref), custom_call_target="tpu_custom_call" | custom-call | tf_op jit(solution)/shard_map/pallas_call | solution.py:547

commit v5 on v4

--- a/solution.py
+++ b/solution.py
@@ -46,7 +46,7 @@
 
 FAR_Z = 4
 N_FAR = (GX - 4 * FAR_Z) * GY
-EARLY_REACH = 6
+EARLY_REACH = 10
 
 
 def is_early(gx, gy):
@@ -62,6 +62,10 @@
     itertools.product(range(4 * FAR_Z, GX), range(GY)),
     key=lambda p: (abs(p[1] // 2 - 4), abs(p[0] % 4 - 2), p),
 )
+
+
+def row_sum(value):
+    return jnp.sum(value, axis=0, keepdims=True)
 
 
 def roll_lanes(value, shift):
@@ -92,6 +96,8 @@
         )
 
     barrier = pltpu.get_barrier_semaphore()
+    for o in GREETED[:2]:
+        pl.semaphore_signal(barrier, inc=1, device_id=offset(*o), device_id_type=MESH)
     for sx in range(2):
         @pl.when(has_edge[sx])
         def _(sx=sx):
@@ -100,7 +106,7 @@
         @pl.when(has_x[sx] & has_y[sy])
         def _(sx=sx, sy=sy):
             pl.semaphore_signal(barrier, inc=1, device_id=at(step[sx], step[sy]), device_id_type=MESH)
-    for o in GREETED:
+    for o in GREETED[2:]:
         pl.semaphore_signal(barrier, inc=1, device_id=offset(*o), device_id_type=MESH)
 
     far, early = z >= FAR_Z, is_early(gx, gy)
@@ -173,6 +179,13 @@
             device_id=at(step[sx], step[sy]), device_id_type=MESH,
         )
 
+    def start_x(m):
+        for sx in range(2):
+            @pl.when(has_x[sx])
+            def _(sx=sx):
+                x_copy(sx, m).start()
+
+    start_x(0)
     for sy in range(2):
         @pl.when(has_y[sy])
         def _(sy=sy):
@@ -181,11 +194,8 @@
         @pl.when(has_x[sx] & has_y[sy])
         def _(sx=sx, sy=sy):
             c_copy(sx, sy).start()
-    for m in range(M):
-        for sx in range(2):
-            @pl.when(has_x[sx])
-            def _(sx=sx, m=m):
-                x_copy(sx, m).start()
+    for m in range(1, M):
+        start_x(m)
 
     def tell(level):
         for o in TOLD[level]:
@@ -250,8 +260,6 @@
 
     pl.semaphore_wait(known.at[0], len(TOLD[0]))
     tell(1)
-    pl.semaphore_wait(known.at[1], len(TOLD[1]))
-    tell(2)
 
     for sy in range(2):
         @pl.when(has_y[sy])
@@ -349,7 +357,7 @@
 
     def early_copy(p):
         return pltpu.make_async_remote_copy(
-            src_ref=total.at[0], dst_ref=direct.at[(gx - 4 * FAR_Z) * GY + gy], send_sem=e_send.at[0], recv_sem=e_recv.at[0],
+            src_ref=total.at[0], dst_ref=direct.at[pl.ds((gx - 4 * FAR_Z) * GY + gy, 1)], send_sem=e_send.at[0], recv_sem=e_recv.at[0],
             device_id=p, device_id_type=MESH,
         )
 
@@ -360,13 +368,13 @@
 
     def y_row(a):
         return pltpu.make_async_remote_copy(
-            src_ref=total.at[0], dst_ref=slots_gy.at[a - 1], send_sem=r_send.at[0], recv_sem=r_recv.at[0],
+            src_ref=total.at[0], dst_ref=slots_gy.at[pl.ds(gy, 1)], send_sem=r_send.at[0], recv_sem=r_recv.at[0],
             device_id=(gx, lax.rem(gy + a, GY)), device_id_type=MESH,
         )
 
     def x_row(a):
         return pltpu.make_async_remote_copy(
-            src_ref=total.at[1], dst_ref=slots_gx.at[gx], send_sem=r_send.at[1], recv_sem=r_recv.at[1],
+            src_ref=total.at[1], dst_ref=slots_gx.at[pl.ds(gx, 1)], send_sem=r_send.at[1], recv_sem=r_recv.at[1],
             device_id=(lax.rem(gx + a, GX), gy), device_id_type=MESH,
         )
 
@@ -376,13 +384,16 @@
             device_id=(gx, lax.rem(gy + 1, GY)), device_id_type=MESH,
         )
 
+    pl.semaphore_wait(known.at[1], len(TOLD[1]))
+    tell(2)
     for a in STAGE_GY:
         y_row(a).start()
-    y_rows = awaited(slots_gy, r_send.at[0], r_recv.at[0])
+    slots_gy[pl.ds(gy, 1)] = acc
+    y_rows = awaited(slots_gy.at[0 : GY - 1], r_send.at[0], r_recv.at[0])
     y_rows.wait_recv()
-    acc = acc + jnp.sum(slots_gy[...], axis=0)
+    acc = row_sum(slots_gy[...])
     total[1] = acc
-    slots_gx[gx] = acc
+    slots_gx[pl.ds(gx, 1)] = acc
 
     def wanted(a):
         return jnp.logical_not(far & is_early(lax.rem(gx + a, GX), gy))
@@ -396,14 +407,14 @@
     @pl.when(early)
     def _():
         awaited(slots_gx.at[0 : 4 * FAR_Z - 1], r_send.at[1], r_recv.at[1]).wait_recv()
-        near_sum = jnp.sum(slots_gx[0 : 4 * FAR_Z], axis=0)
+        near_sum = row_sum(slots_gx[0 : 4 * FAR_Z])
         awaited(direct, e_send.at[0], e_recv.at[0]).wait_recv()
-        total[2] = near_sum + jnp.sum(direct[...], axis=0)
+        total[2] = near_sum + row_sum(direct[...])
 
     @pl.when(jnp.logical_not(early))
     def _():
         awaited(slots_gx.at[0 : GX - 1], r_send.at[1], r_recv.at[1]).wait_recv()
-        total[2] = jnp.sum(slots_gx[...], axis=0)
+        total[2] = row_sum(slots_gx[...])
 
     acc = total[2]
 
@@ -526,9 +537,9 @@
             vmem((M, 2, 8, NK)),
             vmem((len(PAIRS) * M, NK)),
             vmem((3, 1, NK)),
-            vmem((GX, 1, NK)),
-            vmem((GY - 1, 1, NK)),
-            vmem((N_FAR, 1, NK)),
+            vmem((GX, NK)),
+            vmem((GY, NK)),
+            vmem((N_FAR, NK)),
             dma((2, M)),
             dma((2, M)),
             dma((2,)),

time: 30.6 us -> 30.4 us (level)
  no operation moved by 1% of the time
where the time goes in v5:
time: 30.4 us; the launch traced here: 30.2 us
  Pallas kernels  29.6 us (97%)
  between operations  0.64 us (2%)
    pallas_call x1, Pallas kernels, shards(): pl.pallas_call(kernel, out_shape=(pltpu.VMEM(density.shape, F32), pltpu.V...  28.9 us
    pallas_call x1, Pallas kernels, shards(): pl.pallas_call(store, out_shape=(jax.ShapeDtypeStruct(density.shape, F32)...  0.68 us

profile of v5, /device:TPU:1, one launch (start us, length us, event | category | flops | bytes accessed | tf_op | source)
XLA Modules:
  0.0 30.2 jit_solution(4621662752990304783)
XLA Ops:
  0.6 28.9 %shard_map.41 = (f32[4,4,16,128]{3,2,1,0:T(8,128)S(1)}, f32[4,5]{1,0:T(4,128)S(1)}) custom-call(f32[4,4,16,128]{3,2,1,0:T(8,128)} %d_hbm.1, f32[4,9]{1,0:T(4,128)} %rate_hbm.1), custom_call_target="tpu_custom_call" | custom-call | tf_op jit(solution)/shard_map/pallas_call | solution.py:521
  29.5 0.7 %shard_map.42 = (f32[4,4,16,128]{3,2,1,0:T(8,128)}, f32[4,5]{1,0:T(4,128)}) custom-call(f32[4,4,16,128]{3,2,1,0:T(8,128)S(1)} %get-tuple-element.4.field_ref, f32[4,5]{1,0:T(4,128)S(1)} %get-tuple-element.5.entry_ref), custom_call_target="tpu_custom_call" | custom-call | tf_op jit(solution)/shard_map/pallas_call | solution.py:558

commit v6 on v5

--- a/solution.py
+++ b/solution.py
@@ -11,6 +11,7 @@
 MESH = pl.DeviceIdType.MESH
 F32 = jnp.float32
 TAU = 0.01
+TINY = 1e-36
 TAYLOR_TERMS = 16
 SQUARINGS = 4
 M, CI, CJ, NK = 4, 4, 16, 128
@@ -404,6 +405,35 @@
         def _(a=a):
             x_row(a).start()
 
+    y_rows.wait_send()
+
+    @pl.when(far)
+    def _():
+        for p in EARLY:
+            early_copy(p).wait_send()
+        for a in STAGE_GX:
+            @pl.when(wanted(a))
+            def _(a=a):
+                x_row(a).wait_send()
+
+    @pl.when(jnp.logical_not(far))
+    def _():
+        awaited(slots_gx.at[0 : GX - 1], r_send.at[1], r_recv.at[1]).wait_send()
+
+    for sy in range(2):
+        @pl.when(has_y[sy])
+        def _(sy=sy):
+            y_copy(sy).wait_send()
+    for sx, sy in itertools.product((0, 1), (0, 1)):
+        @pl.when(has_x[sx] & has_y[sy])
+        def _(sx=sx, sy=sy):
+            c_copy(sx, sy).wait_send()
+    for m in range(M):
+        for sx in range(2):
+            @pl.when(has_x[sx])
+            def _(sx=sx, m=m):
+                x_copy(sx, m).wait_send()
+
     @pl.when(early)
     def _():
         awaited(slots_gx.at[0 : 4 * FAR_Z - 1], r_send.at[1], r_recv.at[1]).wait_recv()
@@ -424,13 +454,13 @@
     scale = 1.0 / picked[0]
     a1, a2, b11, b12, b22 = [value * scale for value in picked[1:]]
     h00 = a1
-    n1 = b11 - h00 * h00
+    n1 = jnp.maximum(b11 - h00 * h00, TINY)
     h10 = jnp.sqrt(n1)
     e = a2 - h00 * a1
     h01 = e / h10
     h11 = ((b12 - h00 * b11) - h00 * e) / n1
     ss = (b22 - h00 * b12) - h00 * (b12 - h00 * b11)
-    h21 = jnp.sqrt(ss / n1 - h01 * h01 - h11 * h11)
+    h21 = jnp.sqrt(jnp.maximum(ss / n1 - h01 * h01 - h11 * h11, TINY))
 
     step_scale = lam_row * TAU
     entries = [step_scale * h for h in (h00, h10, h01, h11, h21)]
@@ -473,35 +503,6 @@
         s0, s1, s2 = (jnp.broadcast_to(f[:, m : m + 1], (CJ, NK)) for f in (f0, f1, f2))
         for r in range(CI):
             out_ref[m, r] = s0 * d_ref[m, r] + s1 * upad[m, r + 2, 8 : 8 + CJ] + s2 * out_ref[m, r]
-
-    y_rows.wait_send()
-
-    @pl.when(far)
-    def _():
-        for p in EARLY:
-            early_copy(p).wait_send()
-        for a in STAGE_GX:
-            @pl.when(wanted(a))
-            def _(a=a):
-                x_row(a).wait_send()
-
-    @pl.when(jnp.logical_not(far))
-    def _():
-        awaited(slots_gx.at[0 : GX - 1], r_send.at[1], r_recv.at[1]).wait_send()
-
-    for sy in range(2):
-        @pl.when(has_y[sy])
-        def _(sy=sy):
-            y_copy(sy).wait_send()
-    for sx, sy in itertools.product((0, 1), (0, 1)):
-        @pl.when(has_x[sx] & has_y[sy])
-        def _(sx=sx, sy=sy):
-            c_copy(sx, sy).wait_send()
-    for m in range(M):
-        for sx in range(2):
-            @pl.when(has_x[sx])
-            def _(sx=sx, m=m):
-                x_copy(sx, m).wait_send()
 
 
 def store(field_ref, entry_ref, field_out, entry_out, sems):

time: 30.4 us -> 30.2 us (level)
  no operation moved by 1% of the time
where the time goes in v6:
time: 30.2 us; the launch traced here: 30.1 us
  Pallas kernels  29.4 us (97%)
  between operations  0.64 us (2%)
    pallas_call x1, Pallas kernels, shards(): pl.pallas_call(kernel, out_shape=(pltpu.VMEM(density.shape, F32), pltpu.V...  28.7 us
    pallas_call x1, Pallas kernels, shards(): pl.pallas_call(store, out_shape=(jax.ShapeDtypeStruct(density.shape, F32)...  0.68 us

profile of v6, /device:TPU:1, one launch (start us, length us, event | category | flops | bytes accessed | tf_op | source)
XLA Modules:
  0.0 30.1 jit_solution(9909196377939262093)
XLA Ops:
  0.6 28.7 %shard_map.41 = (f32[4,4,16,128]{3,2,1,0:T(8,128)S(1)}, f32[4,5]{1,0:T(4,128)S(1)}) custom-call(f32[4,4,16,128]{3,2,1,0:T(8,128)} %d_hbm.1, f32[4,9]{1,0:T(4,128)} %rate_hbm.1), custom_call_target="tpu_custom_call" | custom-call | tf_op jit(solution)/shard_map/pallas_call | solution.py:522
  29.4 0.7 %shard_map.42 = (f32[4,4,16,128]{3,2,1,0:T(8,128)}, f32[4,5]{1,0:T(4,128)}) custom-call(f32[4,4,16,128]{3,2,1,0:T(8,128)S(1)} %get-tuple-element.4.field_ref, f32[4,5]{1,0:T(4,128)S(1)} %get-tuple-element.5.entry_ref), custom_call_target="tpu_custom_call" | custom-call | tf_op jit(solution)/shard_map/pallas_call | solution.py:559

commit v7 on v6

--- a/solution.py
+++ b/solution.py
@@ -1,5 +1,6 @@
 import functools
 import itertools
+import math
 
 import jax
 import jax.numpy as jnp
@@ -259,6 +260,7 @@
         for r in range(CI):
             dpad[m, r + 2, 8 : 8 + CJ] = d_ref[m, r]
 
+    tables = [coefficients(m) for m in range(M)]
     pl.semaphore_wait(known.at[0], len(TOLD[0]))
     tell(1)
 
@@ -283,7 +285,7 @@
 
     inside_hi = (gx < GX - 1).astype(F32)
     for m in range(M):
-        c, make_u, make_v, gain_j, loss = coefficients(m)
+        c, make_u, make_v, gain_j, loss = tables[m]
         for sx in range(2):
             @pl.when(has_x[sx])
             def _(sx=sx, m=m):
@@ -466,17 +468,29 @@
     entries = [step_scale * h for h in (h00, h10, h01, h11, h21)]
     small = 1.0 / 2.0**SQUARINGS
     g00, g10, g01, g11, g21 = [entry * small for entry in entries]
-    one, zero = jnp.ones_like(h00), jnp.zeros_like(h00)
-    p00, p01, p10, p11 = one, zero, zero, one
-    w0 = w1 = zero
-    for term in range(TAYLOR_TERMS, 0, -1):
-        f = 1.0 / term
-        w0, w1 = g21 * f * p10, g21 * f * p11
-        q00 = 1.0 + (g00 * f * p00 + g01 * f * p10)
-        q01 = g00 * f * p01 + g01 * f * p11
-        q10 = g10 * f * p00 + g11 * f * p10
-        q11 = 1.0 + (g10 * f * p01 + g11 * f * p11)
-        p00, p01, p10, p11 = q00, q01, q10, q11
+
+    def times(left, right):
+        (l00, l01, l10, l11), (r00, r01, r10, r11) = left, right
+        return (
+            l00 * r00 + l01 * r10,
+            l00 * r01 + l01 * r11,
+            l10 * r00 + l11 * r10,
+            l10 * r01 + l11 * r11,
+        )
+
+    g1 = (g00, g01, g10, g11)
+    g2 = times(g1, g1)
+    g3, g4 = times(g2, g1), times(g2, g2)
+    factors = [1.0 / math.factorial(n) for n in range(1, TAYLOR_TERMS + 1)]
+    q = None
+    for start in range(TAYLOR_TERMS - 4, -1, -4):
+        f = factors[start : start + 4]
+        part = [f[1] * a + (f[2] * b + f[3] * c) for a, b, c in zip(g1, g2, g3)]
+        part[0], part[3] = part[0] + f[0], part[3] + f[0]
+        q = part if q is None else [a + b for a, b in zip(part, times(g4, q))]
+    w0, w1 = g21 * q[2], g21 * q[3]
+    p00, p01, p10, p11 = times(g1, q)
+    p00, p11 = 1.0 + p00, 1.0 + p11
     for _ in range(SQUARINGS):
         w0, w1 = w0 + (w0 * p00 + w1 * p10), w1 + (w0 * p01 + w1 * p11)
         q00 = p00 * p00 + p01 * p10

time: 30.2 us -> 30.2 us (level)
  no operation moved by 1% of the time
where the time goes in v7:
time: 30.2 us; the launch traced here: 30 us
  Pallas kernels  29.4 us (97%)
  between operations  0.64 us (2%)
    pallas_call x1, Pallas kernels, shards(): pl.pallas_call(kernel, out_shape=(pltpu.VMEM(density.shape, F32), pltpu.V...  28.7 us
    pallas_call x1, Pallas kernels, shards(): pl.pallas_call(store, out_shape=(jax.ShapeDtypeStruct(density.shape, F32)...  0.68 us

profile of v7, /device:TPU:1, one launch (start us, length us, event | category | flops | bytes accessed | tf_op | source)
XLA Modules:
  0.0 30.0 jit_solution(10152265042077278998)
XLA Ops:
  0.6 28.7 %shard_map.41 = (f32[4,4,16,128]{3,2,1,0:T(8,128)S(1)}, f32[4,5]{1,0:T(4,128)S(1)}) custom-call(f32[4,4,16,128]{3,2,1,0:T(8,128)} %d_hbm.1, f32[4,9]{1,0:T(4,128)} %rate_hbm.1), custom_call_target="tpu_custom_call" | custom-call | tf_op jit(solution)/shard_map/pallas_call | solution.py:536
  29.4 0.7 %shard_map.42 = (f32[4,4,16,128]{3,2,1,0:T(8,128)}, f32[4,5]{1,0:T(4,128)}) custom-call(f32[4,4,16,128]{3,2,1,0:T(8,128)S(1)} %get-tuple-element.4.field_ref, f32[4,5]{1,0:T(4,128)S(1)} %get-tuple-element.5.entry_ref), custom_call_target="tpu_custom_call" | custom-call | tf_op jit(solution)/shard_map/pallas_call | solution.py:573

commit v8 on v6

--- a/solution.py
+++ b/solution.py
@@ -97,16 +97,16 @@
         )
 
     barrier = pltpu.get_barrier_semaphore()
+    for sx, sy in itertools.product((0, 1), (0, 1)):
+        @pl.when(has_x[sx] & has_y[sy])
+        def _(sx=sx, sy=sy):
+            pl.semaphore_signal(barrier, inc=1, device_id=at(step[sx], step[sy]), device_id_type=MESH)
     for o in GREETED[:2]:
         pl.semaphore_signal(barrier, inc=1, device_id=offset(*o), device_id_type=MESH)
     for sx in range(2):
         @pl.when(has_edge[sx])
         def _(sx=sx):
             pl.semaphore_signal(barrier, inc=1, device_id=at(step[sx], 0), device_id_type=MESH)
-    for sx, sy in itertools.product((0, 1), (0, 1)):
-        @pl.when(has_x[sx] & has_y[sy])
-        def _(sx=sx, sy=sy):
-            pl.semaphore_signal(barrier, inc=1, device_id=at(step[sx], step[sy]), device_id_type=MESH)
     for o in GREETED[2:]:
         pl.semaphore_signal(barrier, inc=1, device_id=offset(*o), device_id_type=MESH)
 

time: 30.2 us -> 30.2 us (level)
  no operation moved by 1% of the time
where the time goes in v8:
time: 30.2 us; the launch traced here: 30 us
  Pallas kernels  29.4 us (97%)
  between operations  0.64 us (2%)
    pallas_call x1, Pallas kernels, shards(): pl.pallas_call(kernel, out_shape=(pltpu.VMEM(density.shape, F32), pltpu.V...  28.7 us
    pallas_call x1, Pallas kernels, shards(): pl.pallas_call(store, out_shape=(jax.ShapeDtypeStruct(density.shape, F32)...  0.68 us

profile of v8, /device:TPU:1, one launch (start us, length us, event | category | flops | bytes accessed | tf_op | source)
XLA Modules:
  0.0 30.0 jit_solution(6463230793964631032)
XLA Ops:
  0.6 28.7 %shard_map.41 = (f32[4,4,16,128]{3,2,1,0:T(8,128)S(1)}, f32[4,5]{1,0:T(4,128)S(1)}) custom-call(f32[4,4,16,128]{3,2,1,0:T(8,128)} %d_hbm.1, f32[4,9]{1,0:T(4,128)} %rate_hbm.1), custom_call_target="tpu_custom_call" | custom-call | tf_op jit(solution)/shard_map/pallas_call | solution.py:522
  29.3 0.7 %shard_map.42 = (f32[4,4,16,128]{3,2,1,0:T(8,128)}, f32[4,5]{1,0:T(4,128)}) custom-call(f32[4,4,16,128]{3,2,1,0:T(8,128)S(1)} %get-tuple-element.4.field_ref, f32[4,5]{1,0:T(4,128)S(1)} %get-tuple-element.5.entry_ref), custom_call_target="tpu_custom_call" | custom-call | tf_op jit(solution)/shard_map/pallas_call | solution.py:559
